TPU v7x, 32 devices: a whole 2x2x4 slice. The times are simulated.
32 devices in a mesh: grp: 2 (over y), wk: 8 (over z, x), ar: 2 (over core).
Axes of the slice: x: 2, y: 2, z: 4, core: 2. Of those that a mesh axis runs over, the one named last changes fastest.
Arguments:
- latent: float32 [48, 16, 2048], P('grp', 'wk', 'ar'), parts along dimension 0, may hold values from -3 to 3
- log_offset: float32 [48, 16, 2048], P('grp', 'wk', 'ar'), parts along dimension 0, may hold values from -1 to 1.5
- case_counts: int32 [48, 16, 2048], P('grp', 'wk', 'ar'), parts along dimension 0, may hold values from 0 to 9
- tau: float32 [24], replicated, may hold values from 0.3 to 3
- phi_one: float32 [24], replicated, may hold values from 0.2 to 1.2
- phi_two: float32 [24], replicated, may hold values from -0.5 to 0.3
- blocks: float32 [16, 4, 128, 128], P('ar'), as said below
- block_index: int32 [16, 4], P('ar'), may hold values from 0 to 15, as said below
- block_count: int32 [16], P('ar'), may hold values from 2 to 4, as said below
Outputs:
- updated: float32 [48, 16, 2048], P('grp', 'wk', 'ar'), parts along dimension 0
There are 2 independent parts, one for each index of `grp`. A program takes and returns all parts, laid end to end along the dimension named above; an argument that names none is the same for every part. Nothing has to cross between parts.
Inputs may be any that keep to these rules, and one draw needn't show every extreme that they name: `block_index`: slot 0 of block row b lists b; slots below block_count list distinct blocks within two of b, those of b - 1 and b + 1 that exist always among them; unused slots list b. The pattern is symmetric: row b lists c where row c lists b. `block_count`: some block row uses all 4 slots and some uses 2. `blocks`: the block that row b lists for c is the transpose of the block that row c lists for b; the assembled spatial matrix has entries off the diagonal in [-1 / 512, 1 / 512] and a diagonal larger than the sum of magnitudes of the rest of its row.
All inputs are finite; a program needn't handle non-finite values.
Results may differ from a plain program's by a relative error of at most 0.00023.
Values sent between devices are 32-bit elements; how exact they have to be, the bound alone decides.
A program may use at most 64 MiB of HBM per device.

v0:
```python
import jax
import jax.numpy as jnp
from jax import lax
from jax.sharding import PartitionSpec as P

ITERS = 3


def extended(value, sides, width):
    for axis, dim in sides:
        peers, length = (lax.axis_size(axis), value.shape[dim])
        up = [(i, (i + 1) % peers) for i in range(peers - 1)]
        down = [(j, i) for i, j in up]
        last = lax.slice_in_dim(value, length - width, length, axis=dim)
        initial = lax.slice_in_dim(value, 0, width, axis=dim)
        before = lax.ppermute(last, axis, up)
        after = lax.ppermute(initial, axis, down)
        value = jnp.concatenate([before, value, after], axis=dim)
    return value


def temporal(field, first_lag, second_lag):
    weeks_here = field.shape[1]
    weeks_total = lax.axis_size("wk") * weeks_here
    padded = extended(field, (("wk", 1),), 2)
    innovation = (
        padded[:, 2 : weeks_here + 4]
        - first_lag * padded[:, 1 : weeks_here + 3]
        - second_lag * padded[:, 0 : weeks_here + 2]
    )
    week_number = lax.axis_index("wk") * weeks_here + jnp.arange(weeks_here + 2)
    innovation = jnp.where((week_number < weeks_total)[None, :, None], innovation, 0.0)
    return (
        innovation[:, 0:weeks_here]
        - first_lag * innovation[:, 1 : weeks_here + 1]
        - second_lag * innovation[:, 2 : weeks_here + 2]
    )


def spatial(field, masked, block_index):
    cancers, weeks_here, areas_here = field.shape
    rows_here, slot_total, width, unused = masked.shape
    padded = extended(field, (("ar", 2),), 2 * width)
    first_row = lax.axis_index("ar") * rows_here - 2
    local_index = block_index - first_row
    blocks_of = padded.reshape(cancers, weeks_here, rows_here + 4, width)[:, :, local_index, :]
    result = jnp.einsum("cwnsi,nsij->cwnj", blocks_of, masked, precision=lax.Precision.HIGHEST)
    return result.reshape(cancers, weeks_here, areas_here)


def global_sum(values):
    return lax.psum(values, ("wk", "ar"))[:, None, None]


def local(latent, log_offset, case_counts, tau, phi_one, phi_two, blocks, block_index, block_count):
    slot_live = (jnp.arange(blocks.shape[1])[None, :] < block_count[:, None]).astype(jnp.float32)
    masked = blocks * slot_live[:, :, None, None]
    first_lag = phi_one[:, None, None]
    second_lag = phi_two[:, None, None]
    prior_scale = tau[:, None, None]

    def prior(field):
        return prior_scale * spatial(temporal(field, first_lag, second_lag), masked, block_index)

    mean = jnp.exp(log_offset + latent)
    gradient = case_counts.astype(jnp.float32) - mean - prior(latent)
    search = jnp.zeros_like(latent)
    residual = gradient
    direction = gradient
    norm_now = global_sum(jnp.sum(residual * residual, axis=(1, 2)))
    for iteration in range(ITERS):
        image = prior(direction) + mean * direction
        curve = lax.psum(jnp.sum(direction * image, axis=(1, 2)), ("wk", "ar"))[:, None, None]
        alpha = norm_now / curve
        search = search + alpha * direction
        residual = residual - alpha * image
        norm_next = global_sum(jnp.sum(residual * residual, axis=(1, 2)))
        direction = residual + norm_next / norm_now * direction
        norm_now = norm_next
    return latent + search


def solution(mesh):
    return jax.shard_map(
        local,
        mesh=mesh,
        in_specs=(
            P("grp", "wk", "ar"),
            P("grp", "wk", "ar"),
            P("grp", "wk", "ar"),
            P(),
            P(),
            P(),
            P("ar", None, None, None),
            P("ar", None),
            P("ar"),
        ),
        out_specs=P("grp", "wk", "ar"),
        check_vma=False,
    )
```

profile of v0, /device:TPU:0, one launch (start us, length us, event | category | flops | bytes accessed | tf_op | source)
XLA Modules:
  0.0 239.7 jit_solution(6217665343981666064)
XLA Ops:
  0.0 1.0 copy.32
  1.0 5.0 %collective-permute-start.1 = (f32[24,2,1024]{2,0,1:T(8,128)S(1)}, f32[24,2,1024]{2,0,1:T(8,128)S(1)}, u32[]{:S(2)}, u32[]{:S(2)}) collective-permute-start(f32[24,2,1024]{2,0,1:T(8,128)S(1)} %copy.32), channel_id=1, source_target_pairs={{0,2},{2,4},{4,6},{6,8},{8,10},{10,12},{12,14},{1,3},{3,5},{5,7},{... | collective-permute-start | bytes 589832 | tf_op jit(solution)/shard_map/ppermute | solution.py:16
  6.0 1.3 collective-permute-start
  7.3 0.7 compare_select_fusion
  8.2 0.7 fusion.60
  8.9 1.3 collective-permute-done.1
  10.2 4.0 %collective-permute-done = f32[24,2,1024]{2,0,1:T(8,128)S(1)} collective-permute-done((f32[24,2,1024]{2,0,1:T(8,128)S(1)}, f32[24,2,1024]{2,0,1:T(8,128)S(1)}, u32[]{:S(2)}, u32[]{:S(2)}) %collective-permute-start) | collective-permute-done | bytes 196640 | tf_op jit(solution)/shard_map/ppermute | solution.py:17
  14.3 0.8 fusion.43
  15.1 0.8 fusion.56
  15.9 1.3 collective-permute-start.2
  17.2 1.3 collective-permute-start.3
  18.5 1.8 collective-permute-done.3
  20.3 0.6 gather_fusion
  21.0 1.5 fusion.12
  22.8 4.5 %collective-permute-start.5 = (f32[24,2,1024]{2,0,1:T(8,128)S(1)}, f32[24,2,1024]{2,0,1:T(8,128)S(1)}, u32[]{:S(2)}, u32[]{:S(2)}) collective-permute-start(f32[24,2,1024]{2,0,1:T(8,128)S(1)} %get-tuple-element.13), channel_id=1, source_target_pairs={{0,2},{2,4},{4,6},{6,8},{8,10},{10,12},{12,14},{1,3},{3,5},{5,7},{... | collective-permute-start | bytes 589832 | tf_op jit(solution)/shard_map/ppermute | solution.py:16
  27.3 1.3 collective-permute-start.4
  28.6 3.2 %collective-permute-done.5 = f32[24,2,1024]{2,0,1:T(8,128)S(1)} collective-permute-done((f32[24,2,1024]{2,0,1:T(8,128)S(1)}, f32[24,2,1024]{2,0,1:T(8,128)S(1)}, u32[]{:S(2)}, u32[]{:S(2)}) %collective-permute-start.5) | collective-permute-done | bytes 196640 | tf_op jit(solution)/shard_map/ppermute | solution.py:16
  31.7 5.5 %collective-permute-done.4 = f32[24,2,1024]{2,0,1:T(8,128)S(1)} collective-permute-done((f32[24,2,1024]{2,0,1:T(8,128)S(1)}, f32[24,2,1024]{2,0,1:T(8,128)S(1)}, u32[]{:S(2)}, u32[]{:S(2)}) %collective-permute-start.4) | collective-permute-done | bytes 196640 | tf_op jit(solution)/shard_map/ppermute | solution.py:17
  37.5 1.3 collective-permute-start.6
  38.8 1.3 collective-permute-start.7
  40.1 1.8 collective-permute-done.7
  41.9 1.5 gather_fusion.1
  43.4 2.6 %fusion.15 = f32[8,2,3,8,128]{4,3,2,1,0:T(8,128)S(1)} fusion(f32[24,2,8,4,128]{4,0,1,3,2:T(8,128)} %bitcast.120, f32[8,4,128,128]{3,2,1,0:T(8,128)S(1)} %copy-done, f32[8,4]{1,0:T(8,128)S(1)} %fusion.60), kind=kOutput, calls=%fused_computation.17 | convolution fusion | flops 302514176 | bytes 3080320 | tf_op jit(solution)/shard_map/cwnsi,nsij->cwnj/dot_general | solution.py:47
  46.2 34.6 %all-reduce = (f32[24]{0:T(128)S(1)}, f32[24]{0:T(128)S(1)}) all-reduce(f32[24]{0:T(128)S(1)} %get-tuple-element.6, f32[24]{0:T(128)S(1)} %get-tuple-element.5), channel_id=1, replica_groups=mesh['grp'=2,'wk'=8,'ar'=2] {'wk','ar'}, use_global_device_ids=true, to_apply=%region_1.2 | all-reduce | flops 48 | bytes 384 | tf_op jit(solution)/shard_map/psum | solution.py:52
  80.9 0.2 multiply_reduce_fusion.2
  81.1 29.5 %psum.44 = f32[24]{0:T(128)S(1)} all-reduce(f32[24]{0:T(128)S(1)} %get-tuple-element.11), channel_id=1, replica_groups=mesh['grp'=2,'wk'=8,'ar'=2] {'wk','ar'}, use_global_device_ids=true, to_apply=%region_5.6 | all-reduce | flops 24 | bytes 192 | tf_op jit(solution)/shard_map/psum | solution.py:52
  110.7 1.3 collective-permute-start.9
  112.0 1.3 collective-permute-start.8
  113.3 7.4 %collective-permute-done.9 = f32[24,2,1024]{2,0,1:T(8,128)S(1)} collective-permute-done((f32[24,2,1024]{2,0,1:T(8,128)S(1)}, f32[24,2,1024]{2,0,1:T(8,128)S(1)}, u32[]{:S(2)}, u32[]{:S(2)}) %collective-permute-start.9) | collective-permute-done | bytes 196640 | tf_op jit(solution)/shard_map/ppermute | solution.py:16
  120.9 1.7 collective-permute-start.10
  122.6 1.3 collective-permute-start.11
  124.0 1.8 collective-permute-done.11
  125.8 1.5 gather_fusion.2
  127.3 2.7 %fusion.18 = f32[8,2,3,8,128]{4,3,2,1,0:T(8,128)S(1)} fusion(f32[24,2,8,4,128]{4,0,1,3,2:T(8,128)} %bitcast.121, f32[8,4,128,128]{3,2,1,0:T(8,128)S(1)} %copy-done, f32[8,4]{1,0:T(8,128)S(1)} %fusion.60), kind=kOutput, calls=%fused_computation.18 | convolution fusion | flops 302514176 | bytes 3080320 | tf_op jit(solution)/shard_map/cwnsi,nsij->cwnj/dot_general | solution.py:47
  130.0 0.2 multiply_reduce_fusion.1
  130.2 29.6 %psum.45 = f32[24]{0:T(128)S(1)} all-reduce(f32[24]{0:T(128)S(1)} %get-tuple-element.9), channel_id=1, replica_groups=mesh['grp'=2,'wk'=8,'ar'=2] {'wk','ar'}, use_global_device_ids=true, to_apply=%region_7.8 | all-reduce | flops 24 | bytes 192 | tf_op jit(solution)/shard_map/psum | solution.py:73
  159.8 0.2 multiply_reduce_fusion
  160.1 29.5 %psum.46 = f32[24]{0:T(128)S(1)} all-reduce(f32[24]{0:T(128)S(1)} %multiply_reduce_fusion), channel_id=1, replica_groups=mesh['grp'=2,'wk'=8,'ar'=2] {'wk','ar'}, use_global_device_ids=true, to_apply=%region_9.10 | all-reduce | flops 24 | bytes 192 | tf_op jit(solution)/shard_map/psum | solution.py:52
  189.7 1.3 collective-permute-start.13
  191.0 1.3 collective-permute-start.12
  192.3 7.4 %collective-permute-done.13 = f32[24,2,1024]{2,0,1:T(8,128)S(1)} collective-permute-done((f32[24,2,1024]{2,0,1:T(8,128)S(1)}, f32[24,2,1024]{2,0,1:T(8,128)S(1)}, u32[]{:S(2)}, u32[]{:S(2)}) %collective-permute-start.13) | collective-permute-done | bytes 196640 | tf_op jit(solution)/shard_map/ppermute | solution.py:16
  199.9 1.7 collective-permute-start.14
  201.6 1.3 collective-permute-start.15
  202.9 1.8 collective-permute-done.15
  204.7 1.5 gather_fusion.3
  206.2 2.7 %fusion.21 = f32[8,2,3,8,128]{4,3,2,1,0:T(8,128)S(1)} fusion(f32[24,2,8,4,128]{4,0,1,3,2:T(8,128)} %bitcast.118, f32[8,4,128,128]{3,2,1,0:T(8,128)S(1)} %copy-done, f32[8,4]{1,0:T(8,128)S(1)} %fusion.60), kind=kOutput, calls=%fused_computation.19 | convolution fusion | flops 302514176 | bytes 3080320 | tf_op jit(solution)/shard_map/cwnsi,nsij->cwnj/dot_general | solution.py:47
  209.1 29.6 %psum.47 = f32[24]{0:T(128)S(1)} all-reduce(f32[24]{0:T(128)S(1)} %fusion.46), channel_id=1, replica_groups=mesh['grp'=2,'wk'=8,'ar'=2] {'wk','ar'}, use_global_device_ids=true, to_apply=%region_11.12 | all-reduce | flops 24 | bytes 192 | tf_op jit(solution)/shard_map/psum | solution.py:73
  238.9 0.8 copy.33
  (51 shorter events, 2.0 us)
Async XLA Ops:
  1.0 20.0 %copy-start = (f32[8,4,128,128]{3,2,1,0:T(8,128)S(1)}, f32[8,4,128,128]{3,2,1,0:T(8,128)}, u32[]{:S(2)}) copy-start(f32[8,4,128,128]{3,2,1,0:T(8,128)} %param.15) | copy-start | bytes 6291460
  1.0 9.2 %collective-permute-start.1 = (f32[24,2,1024]{2,0,1:T(8,128)S(1)}, f32[24,2,1024]{2,0,1:T(8,128)S(1)}, u32[]{:S(2)}, u32[]{:S(2)}) collective-permute-start(f32[24,2,1024]{2,0,1:T(8,128)S(1)} %copy.32), channel_id=1, source_target_pairs={{0,2},{2,4},{4,6},{6,8},{8,10},{10,12},{12,14},{1,3},{3,5},{5,7},{... | collective-permute-start | bytes 589832 | tf_op jit(solution)/shard_map/ppermute | solution.py:16
  6.0 8.3 %collective-permute-start = (f32[24,2,1024]{2,0,1:T(8,128)S(1)}, f32[24,2,1024]{2,0,1:T(8,128)S(1)}, u32[]{:S(2)}, u32[]{:S(2)}) collective-permute-start(f32[24,2,1024]{2,0,1:T(8,128)S(1)} %copy.32), channel_id=1, source_target_pairs={{2,0},{4,2},{6,4},{8,6},{10,8},{12,10},{14,12},{3,1},{5,3},{7,5},{... | collective-permute-start | bytes 589832 | tf_op jit(solution)/shard_map/ppermute | solution.py:17
  15.9 2.6 %collective-permute-start.2 = (f32[24,2,256]{2,0,1:T(8,128)S(1)}, f32[24,2,256]{2,0,1:T(8,128)S(1)}, u32[]{:S(2)}, u32[]{:S(2)}) collective-permute-start(f32[24,2,256]{2,0,1:T(8,128)S(1)} %get-tuple-element.21), channel_id=1, source_target_pairs={{0,1},{2,3},{4,5},{6,7},{8,9},{10,11},{12,13},{14,15},{16,17},{18,... | collective-permute-start | bytes 147464 | tf_op jit(solution)/shard_map/ppermute | solution.py:16
  17.2 3.1 %collective-permute-start.3 = (f32[24,2,256]{2,0,1:T(8,128)S(1)}, f32[24,2,256]{2,0,1:T(8,128)S(1)}, u32[]{:S(2)}, u32[]{:S(2)}) collective-permute-start(f32[24,2,256]{2,0,1:T(8,128)S(1)} %get-tuple-element.22), channel_id=1, source_target_pairs={{1,0},{3,2},{5,4},{7,6},{9,8},{11,10},{13,12},{15,14},{17,16},{19,... | collective-permute-start | bytes 147464 | tf_op jit(solution)/shard_map/ppermute | solution.py:17
  20.3 2.2 copy-start.1
  20.3 2.2 copy-start.7
  20.9 1.6 copy-start.3
  21.0 1.6 copy-start.4
  21.0 16.2 %copy-start.5 = (f32[24]{0:T(128)S(1)}, f32[24]{0:T(128)}, u32[]{:S(2)}) copy-start(f32[24]{0:T(128)} %param.14) | copy-start | bytes 292
  21.0 16.2 %copy-start.6 = (f32[24]{0:T(128)S(1)}, f32[24]{0:T(128)}, u32[]{:S(2)}) copy-start(f32[24]{0:T(128)} %param.13) | copy-start | bytes 292
  22.8 9.0 %collective-permute-start.5 = (f32[24,2,1024]{2,0,1:T(8,128)S(1)}, f32[24,2,1024]{2,0,1:T(8,128)S(1)}, u32[]{:S(2)}, u32[]{:S(2)}) collective-permute-start(f32[24,2,1024]{2,0,1:T(8,128)S(1)} %get-tuple-element.13), channel_id=1, source_target_pairs={{0,2},{2,4},{4,6},{6,8},{8,10},{10,12},{12,14},{1,3},{3,5},{5,7},{... | collective-permute-start | bytes 589832 | tf_op jit(solution)/shard_map/ppermute | solution.py:16
  27.3 9.9 %collective-permute-start.4 = (f32[24,2,1024]{2,0,1:T(8,128)S(1)}, f32[24,2,1024]{2,0,1:T(8,128)S(1)}, u32[]{:S(2)}, u32[]{:S(2)}) collective-permute-start(f32[24,2,1024]{2,0,1:T(8,128)S(1)} %get-tuple-element.13), channel_id=1, source_target_pairs={{2,0},{4,2},{6,4},{8,6},{10,8},{12,10},{14,12},{3,1},{5,3},{7,5},{... | collective-permute-start | bytes 589832 | tf_op jit(solution)/shard_map/ppermute | solution.py:17
  37.5 2.6 %collective-permute-start.6 = (f32[24,2,256]{2,0,1:T(8,128)S(1)}, f32[24,2,256]{2,0,1:T(8,128)S(1)}, u32[]{:S(2)}, u32[]{:S(2)}) collective-permute-start(f32[24,2,256]{2,0,1:T(8,128)S(1)} %get-tuple-element.19), channel_id=1, source_target_pairs={{0,1},{2,3},{4,5},{6,7},{8,9},{10,11},{12,13},{14,15},{16,17},{18,... | collective-permute-start | bytes 147464 | tf_op jit(solution)/shard_map/ppermute | solution.py:16
  38.8 3.1 %collective-permute-start.7 = (f32[24,2,256]{2,0,1:T(8,128)S(1)}, f32[24,2,256]{2,0,1:T(8,128)S(1)}, u32[]{:S(2)}, u32[]{:S(2)}) collective-permute-start(f32[24,2,256]{2,0,1:T(8,128)S(1)} %get-tuple-element.20), channel_id=1, source_target_pairs={{1,0},{3,2},{5,4},{7,6},{9,8},{11,10},{13,12},{15,14},{17,16},{19,... | collective-permute-start | bytes 147464 | tf_op jit(solution)/shard_map/ppermute | solution.py:17
  110.7 10.0 %collective-permute-start.9 = (f32[24,2,1024]{2,0,1:T(8,128)S(1)}, f32[24,2,1024]{2,0,1:T(8,128)S(1)}, u32[]{:S(2)}, u32[]{:S(2)}) collective-permute-start(f32[24,2,1024]{2,0,1:T(8,128)S(1)} %multiply_add_fusion.1), channel_id=1, source_target_pairs={{0,2},{2,4},{4,6},{6,8},{8,10},{10,12},{12,14},{1,3},{3,5},{5,7},{... | collective-permute-start | bytes 589832 | tf_op jit(solution)/shard_map/ppermute | solution.py:16
  112.0 8.7 %collective-permute-start.8 = (f32[24,2,1024]{2,0,1:T(8,128)S(1)}, f32[24,2,1024]{2,0,1:T(8,128)S(1)}, u32[]{:S(2)}, u32[]{:S(2)}) collective-permute-start(f32[24,2,1024]{2,0,1:T(8,128)S(1)} %multiply_add_fusion.1), channel_id=1, source_target_pairs={{2,0},{4,2},{6,4},{8,6},{10,8},{12,10},{14,12},{3,1},{5,3},{7,5},{... | collective-permute-start | bytes 589832 | tf_op jit(solution)/shard_map/ppermute | solution.py:17
  120.9 3.0 %collective-permute-start.10 = (f32[24,2,256]{2,0,1:T(8,128)S(1)}, f32[24,2,256]{2,0,1:T(8,128)S(1)}, u32[]{:S(2)}, u32[]{:S(2)}) collective-permute-start(f32[24,2,256]{2,0,1:T(8,128)S(1)} %get-tuple-element.17), channel_id=1, source_target_pairs={{0,1},{2,3},{4,5},{6,7},{8,9},{10,11},{12,13},{14,15},{16,17},{18,... | collective-permute-start | bytes 147464 | tf_op jit(solution)/shard_map/ppermute | solution.py:16
  122.6 3.1 %collective-permute-start.11 = (f32[24,2,256]{2,0,1:T(8,128)S(1)}, f32[24,2,256]{2,0,1:T(8,128)S(1)}, u32[]{:S(2)}, u32[]{:S(2)}) collective-permute-start(f32[24,2,256]{2,0,1:T(8,128)S(1)} %get-tuple-element.18), channel_id=1, source_target_pairs={{1,0},{3,2},{5,4},{7,6},{9,8},{11,10},{13,12},{15,14},{17,16},{19,... | collective-permute-start | bytes 147464 | tf_op jit(solution)/shard_map/ppermute | solution.py:17
  189.7 10.0 %collective-permute-start.13 = (f32[24,2,1024]{2,0,1:T(8,128)S(1)}, f32[24,2,1024]{2,0,1:T(8,128)S(1)}, u32[]{:S(2)}, u32[]{:S(2)}) collective-permute-start(f32[24,2,1024]{2,0,1:T(8,128)S(1)} %multiply_add_fusion), channel_id=1, source_target_pairs={{0,2},{2,4},{4,6},{6,8},{8,10},{10,12},{12,14},{1,3},{3,5},{5,7},{... | collective-permute-start | bytes 589832 | tf_op jit(solution)/shard_map/ppermute | solution.py:16
  191.0 8.7 %collective-permute-start.12 = (f32[24,2,1024]{2,0,1:T(8,128)S(1)}, f32[24,2,1024]{2,0,1:T(8,128)S(1)}, u32[]{:S(2)}, u32[]{:S(2)}) collective-permute-start(f32[24,2,1024]{2,0,1:T(8,128)S(1)} %multiply_add_fusion), channel_id=1, source_target_pairs={{2,0},{4,2},{6,4},{8,6},{10,8},{12,10},{14,12},{3,1},{5,3},{7,5},{... | collective-permute-start | bytes 589832 | tf_op jit(solution)/shard_map/ppermute | solution.py:17
  199.9 3.0 %collective-permute-start.14 = (f32[24,2,256]{2,0,1:T(8,128)S(1)}, f32[24,2,256]{2,0,1:T(8,128)S(1)}, u32[]{:S(2)}, u32[]{:S(2)}) collective-permute-start(f32[24,2,256]{2,0,1:T(8,128)S(1)} %get-tuple-element.15), channel_id=1, source_target_pairs={{0,1},{2,3},{4,5},{6,7},{8,9},{10,11},{12,13},{14,15},{16,17},{18,... | collective-permute-start | bytes 147464 | tf_op jit(solution)/shard_map/ppermute | solution.py:16
  201.6 3.1 %collective-permute-start.15 = (f32[24,2,256]{2,0,1:T(8,128)S(1)}, f32[24,2,256]{2,0,1:T(8,128)S(1)}, u32[]{:S(2)}, u32[]{:S(2)}) collective-permute-start(f32[24,2,256]{2,0,1:T(8,128)S(1)} %get-tuple-element.16), channel_id=1, source_target_pairs={{1,0},{3,2},{5,4},{7,6},{9,8},{11,10},{13,12},{15,14},{17,16},{19,... | collective-permute-start | bytes 147464 | tf_op jit(solution)/shard_map/ppermute | solution.py:17
  206.2 32.6 %copy-start.2 = (f32[24,2,1024]{2,1,0:T(2,128)S(1)}, f32[24,2,1024]{2,1,0:T(2,128)}, u32[]{:S(2)}) copy-start(f32[24,2,1024]{2,1,0:T(2,128)} %param.9) | copy-start | bytes 589828
where the time goes:
time: 240 us
  blocking collectives  153 us (64%)
  waiting for transfers between devices  35.9 us (15%)
  starting transfers between devices  28.4 us (12%)
  matrix products  9.54 us (4%)
  local copies, waits for them, and re-layouts  7.11 us (3%)
  other arithmetic  5.42 us (2%)
    psum x3, blocking collectives, global_sum(): return lax.psum(values, ('wk', 'ar'))[:, None, None]  93.6 us
    psum x2, blocking collectives, local(): lax.psum(jnp.sum(direction * image, axis=(1, 2)), ('wk', 'ar'))  59.3 us
    ppermute x8, waiting for transfers between devices, extended(): before = lax.ppermute(last, axis, up)  19.2 us
    ppermute x8, starting transfers between devices, extended(): before = lax.ppermute(last, axis, up)  18.1 us
    ppermute x8, waiting for transfers between devices, extended(): after = lax.ppermute(initial, axis, down)  16.7 us
    ppermute x8, starting transfers between devices, extended(): after = lax.ppermute(initial, axis, down)  10.3 us
    dot_general x4, matrix products, spatial(): jnp.einsum('cwnsi,nsij->cwnj', blocks_of, masked, precision=lax.Precision...  9.54 us
    gather x4, local copies, waits for them, and re-layouts, spatial(): padded.reshape(cancers, weeks_here, rows_here + 4, width)  5.04 us
  transfers between devices with their start and end apart: 16, of which 10 were waited for; matrix products, arithmetic and copies ran while one was open for 1% of the time, Pallas kernels for 0%

commit v1 on v0

--- a/solution.py
+++ b/solution.py
@@ -1,9 +1,14 @@
+import functools
+
 import jax
 import jax.numpy as jnp
 from jax import lax
+from jax.experimental import pallas as pl
+from jax.experimental.pallas import tpu as pltpu
 from jax.sharding import PartitionSpec as P
 
 ITERS = 3
+MESH = pl.DeviceIdType.MESH
 
 
 def extended(value, sides, width):
@@ -80,9 +85,292 @@
     return latent + search
 
 
+def site_kernel(
+    peers, areas, per_chip, weeks_here, rows_here, slot_total,
+    latent, log_offset, case_counts, tau, phi_one, phi_two, blocks, slot_index, slot_count,
+    out,
+    packed, field, matrix, wide, index_all, count_all,
+    temporal_rows, operand, product, mean, direction, residual, search, outgoing, returned,
+    send_sem, recv_sem, matrix_sem, table_sem, back_sem, return_sem,
+):
+    me = lax.axis_index("wk")
+    half = lax.axis_index("ar")
+    width = blocks.shape[-1]
+    site_slots = -(-per_chip // areas)
+    weeks = peers * weeks_here
+    rows = areas * rows_here
+    sites_here = jnp.minimum(site_slots, per_chip - half * site_slots)
+
+    barrier = pltpu.get_barrier_semaphore()
+    for step in range(1, peers * areas):
+        other = lax.rem(me * areas + half + step, peers * areas)
+        pl.semaphore_signal(
+            barrier, inc=1, device_id={"wk": other // areas, "ar": lax.rem(other, areas)}, device_id_type=MESH
+        )
+
+    own_rows = pl.ds(half * rows_here, rows_here)
+    own_matrix = pltpu.make_async_copy(blocks, matrix.at[own_rows], matrix_sem.at[0])
+    own_matrix.start()
+    own_index = pltpu.make_async_copy(slot_index, index_all.at[half], table_sem.at[0])
+    own_index.start()
+    own_count = pltpu.make_async_copy(slot_count, count_all.at[half], table_sem.at[1])
+    own_count.start()
+
+    for site in range(peers * per_chip):
+        for week in range(weeks_here):
+            row = pl.ds(site * rows_here * weeks_here + week, rows_here, stride=weeks_here)
+            now = latent[row, :]
+            rate = jnp.exp(log_offset[row, :] + now)
+            packed[site, 0, week] = now
+            packed[site, 1, week] = rate
+            packed[site, 2, week] = case_counts[row, :].astype(jnp.float32) - rate
+
+    pl.semaphore_wait(barrier, peers * areas - 1)
+
+    twin = {"ar": 1 - half}
+    twin_rows = pl.ds((1 - half) * rows_here, rows_here)
+    to_twin = [
+        pltpu.make_async_remote_copy(
+            slot_index, index_all.at[half], table_sem.at[2], table_sem.at[3], device_id=twin, device_id_type=MESH
+        ),
+        pltpu.make_async_remote_copy(
+            slot_count, count_all.at[half], table_sem.at[4], table_sem.at[5], device_id=twin, device_id_type=MESH
+        ),
+        pltpu.make_async_remote_copy(
+            blocks, matrix.at[own_rows], matrix_sem.at[1], matrix_sem.at[2], device_id=twin, device_id_type=MESH
+        ),
+    ]
+    for copy in to_twin:
+        copy.start()
+
+    def scatter(j, step, starting):
+        core, slot = j // site_slots, j % site_slots
+        peer = lax.rem(me + step, peers)
+        site = peer * per_chip + j
+        source, target = packed.at[site], field.at[slot, me, half]
+        arrived = recv_sem.at[slot, me, half]
+
+        def away():
+            copy = pltpu.make_async_remote_copy(
+                source, target, send_sem.at[j, step], arrived,
+                device_id={"wk": peer, "ar": core}, device_id_type=MESH,
+            )
+            copy.start() if starting else copy.wait_send()
+
+        def here():
+            pltpu.make_async_copy(source, target, arrived).start()
+
+        if step == 0:
+            pl.when(half != core)(away)
+            if starting:
+                pl.when(half == core)(here)
+        else:
+            away()
+
+    for j in range(per_chip):
+        for step in range(peers):
+            scatter(j, step, True)
+
+    def spread(block_row):
+        for slot in range(slot_total):
+            live = slot < count_all[block_row // rows_here, lax.rem(block_row, rows_here)]
+            block = jnp.where(live, matrix[block_row, slot], 0.0)
+            high = block.astype(jnp.bfloat16)
+            low = (block - high.astype(jnp.float32)).astype(jnp.bfloat16)
+            wide[block_row, slot * width : (slot + 1) * width, 0:width] = high
+            wide[block_row, slot * width : (slot + 1) * width, width : 2 * width] = low
+
+    own_matrix.wait()
+    own_index.wait()
+    own_count.wait()
+
+    @pl.loop(0, rows_here)
+    def _(n):
+        spread(half * rows_here + n)
+
+    for copy in to_twin:
+        copy.wait_recv()
+
+    @pl.loop(0, rows_here)
+    def _(n):
+        spread((1 - half) * rows_here + n)
+
+    def prior(first_lag, second_lag):
+        for a in range(areas):
+            part = [direction[pl.ds(t * rows + a * rows_here, rows_here), :] for t in range(weeks)]
+            inner = []
+            for t in range(weeks):
+                value = part[t]
+                if t >= 1:
+                    value = value - first_lag * part[t - 1]
+                if t >= 2:
+                    value = value - second_lag * part[t - 2]
+                inner.append(value)
+            for t in range(weeks):
+                value = inner[t]
+                if t + 1 < weeks:
+                    value = value - first_lag * inner[t + 1]
+                if t + 2 < weeks:
+                    value = value - second_lag * inner[t + 2]
+                temporal_rows[pl.ds(t * rows + a * rows_here, rows_here), :] = value
+        for g in range(rows):
+            value = temporal_rows[pl.ds(g, weeks, stride=rows), :]
+            high = value.astype(jnp.bfloat16)
+            operand[g, 0:weeks] = high
+            operand[g, weeks : 2 * weeks] = (value - high.astype(jnp.float32)).astype(jnp.bfloat16)
+        for n in range(rows):
+            a, b = n // rows_here, n % rows_here
+            left = jnp.concatenate([operand[index_all[a, s, b]] for s in range(slot_total)], axis=1)
+            both = jnp.dot(left, wide[n], preferred_element_type=jnp.float32)
+            value = both[0:weeks, 0:width] + (both[0:weeks, width:] + both[weeks:, 0:width])
+            product[pl.ds(n, weeks, stride=rows), :] = value
+
+    def total(values):
+        return jnp.sum(values, axis=(0, 1), keepdims=True)
+
+    def give(slot, step, a, starting):
+        peer = lax.rem(me + step, peers)
+        source = outgoing.at[slot, peer, a]
+        site = me * per_chip + half * site_slots + slot
+        target, arrived = returned.at[site], return_sem.at[site]
+
+        def away():
+            copy = pltpu.make_async_remote_copy(
+                source, target, back_sem.at[slot, step, a], arrived,
+                device_id={"wk": peer, "ar": a}, device_id_type=MESH,
+            )
+            copy.start() if starting else copy.wait_send()
+
+        def here():
+            pltpu.make_async_copy(source, target, arrived).start()
+
+        if step == 0:
+            pl.when(half != a)(away)
+            if starting:
+                pl.when(half == a)(here)
+        else:
+            away()
+
+    @pl.loop(0, sites_here)
+    def _(slot):
+        site = me * per_chip + half * site_slots + slot
+        scale, first_lag, second_lag = tau[site], phi_one[site], phi_two[site]
+        for w in range(peers):
+            for a in range(areas):
+                pltpu.make_async_copy(packed.at[0], field.at[slot, w, a], recv_sem.at[slot, w, a]).wait()
+        for w in range(peers):
+            for a in range(areas):
+                for t in range(weeks_here):
+                    row = pl.ds((w * weeks_here + t) * rows + a * rows_here, rows_here)
+                    direction[row, :] = field[slot, w, a, 0, t]
+                    mean[row, :] = field[slot, w, a, 1, t]
+                    residual[row, :] = field[slot, w, a, 2, t]
+        prior(first_lag, second_lag)
+        gradient = residual[...] - scale * product[...]
+        residual[...] = gradient
+        direction[...] = gradient
+        search[...] = jnp.zeros_like(gradient)
+
+        def iteration(_, norm_now):
+            prior(first_lag, second_lag)
+            image = scale * product[...] + mean[...] * direction[...]
+            alpha = norm_now / total(direction[...] * image)
+            search[...] += alpha * direction[...]
+            after = residual[...] - alpha * image
+            residual[...] = after
+            norm_next = total(after * after)
+            direction[...] = after + (norm_next / norm_now) * direction[...]
+            return norm_next
+
+        lax.fori_loop(0, ITERS, iteration, total(gradient * gradient))
+        for w in range(peers):
+            for a in range(areas):
+                for t in range(weeks_here):
+                    row = pl.ds((w * weeks_here + t) * rows + a * rows_here, rows_here)
+                    outgoing[slot, w, a, t] = search[row, :]
+        for step in range(peers):
+            for a in range(areas):
+                give(slot, step, a, True)
+
+    for j in range(per_chip):
+        for w in range(peers):
+            site = w * per_chip + j
+            pltpu.make_async_copy(outgoing.at[0, 0, 0], returned.at[site], return_sem.at[site]).wait()
+            for week in range(weeks_here):
+                row = pl.ds(site * rows_here * weeks_here + week, rows_here, stride=weeks_here)
+                out[row, :] = latent[row, :] + returned[site, week]
+
+    for copy in to_twin:
+        copy.wait_send()
+    for j in range(per_chip):
+        for step in range(peers):
+            scatter(j, step, False)
+
+    @pl.loop(0, sites_here)
+    def _(slot):
+        for step in range(peers):
+            for a in range(areas):
+                give(slot, step, a, False)
+
+
+def by_site(
+    peers, areas, latent, log_offset, case_counts, tau, phi_one, phi_two, blocks, block_index, block_count
+):
+    cancers, weeks_here, areas_here = latent.shape
+    rows_here, slot_total, width, _ = blocks.shape
+    if cancers % peers or areas != 2 or rows_here % 8 or (peers * weeks_here) % 16:
+        return local(latent, log_offset, case_counts, tau, phi_one, phi_two, blocks, block_index, block_count)
+    per_chip = cancers // peers
+    site_slots = -(-per_chip // areas)
+    weeks, rows = peers * weeks_here, areas * rows_here
+
+    def as_rows(value):
+        split = value.reshape(cancers, weeks_here, rows_here, width)
+        return split.transpose(0, 2, 1, 3).reshape(cancers * rows_here * weeks_here, width)
+
+    f32, bf16 = jnp.float32, jnp.bfloat16
+    tile = (weeks_here, rows_here, width)
+    plane = pltpu.VMEM((weeks * rows, width), f32)
+    dma = pltpu.SemaphoreType.DMA
+    vmem, smem = pl.BlockSpec(memory_space=pltpu.VMEM), pl.BlockSpec(memory_space=pltpu.SMEM)
+    result = pl.pallas_call(
+        functools.partial(site_kernel, peers, areas, per_chip, weeks_here, rows_here, slot_total),
+        out_shape=jax.ShapeDtypeStruct((cancers * rows_here * weeks_here, width), f32),
+        in_specs=[vmem] * 3 + [smem] * 3 + [pl.BlockSpec(memory_space=pl.ANY)] + [smem] * 2,
+        out_specs=vmem,
+        scratch_shapes=[
+            pltpu.VMEM((cancers, 3) + tile, f32),
+            pltpu.VMEM((site_slots, peers, areas, 3) + tile, f32),
+            pltpu.VMEM((rows, slot_total, width, width), f32),
+            pltpu.VMEM((rows, slot_total * width, 2 * width), bf16),
+            pltpu.SMEM((areas, slot_total, rows_here), jnp.int32),
+            pltpu.SMEM((areas, rows_here), jnp.int32),
+            plane,
+            pltpu.VMEM((rows, 2 * weeks, width), bf16),
+            plane, plane, plane, plane, plane,
+            pltpu.VMEM((site_slots, peers, areas) + tile, f32),
+            pltpu.VMEM((cancers,) + tile, f32),
+            dma((per_chip, peers)),
+            dma((site_slots, peers, areas)),
+            dma((3,)),
+            dma((6,)),
+            dma((site_slots, peers, areas)),
+            dma((cancers,)),
+        ],
+        compiler_params=pltpu.CompilerParams(
+            collective_id=0, has_side_effects=True, vmem_limit_bytes=40 * 1024 * 1024
+        ),
+    )(
+        as_rows(latent), as_rows(log_offset), as_rows(case_counts), tau, phi_one, phi_two,
+        blocks, block_index.T, block_count,
+    )
+    split = result.reshape(cancers, rows_here, weeks_here, width).transpose(0, 2, 1, 3)
+    return split.reshape(latent.shape)
+
+
 def solution(mesh):
     return jax.shard_map(
-        local,
+        functools.partial(by_site, mesh.shape["wk"], mesh.shape["ar"]),
         mesh=mesh,
         in_specs=(
             P("grp", "wk", "ar"),

time: 240 us -> 40.3 us (0.17)
  blocking collectives: 153 us -> 0 us
  waiting for transfers between devices: 35.9 us -> 0 us
  Pallas kernels: 0 us -> 31.7 us
  starting transfers between devices: 28.4 us -> 0 us
  matrix products: 9.54 us -> 0 us
  other arithmetic: 5.42 us -> 0 us
    psum x5 -> x0, blocking collectives: 153 us -> none  [the longest x3 93.6 us: global_sum(): return lax.psum(values, ('wk', 'ar'))[:, None, None]]
    ppermute x16 -> x0, waiting for transfers between devices: 35.9 us -> none  [the longest x8 19.2 us: extended(): before = lax.ppermute(last, axis, up)]
    pallas_call x0 -> x1, Pallas kernels: none -> 31.7 us  [by_site(): pl.pallas_call(functools.partial(site_kernel, peers, areas, per_chip, wee...]
    ppermute x16 -> x0, starting transfers between devices: 28.4 us -> none  [the longest x8 18.1 us: extended(): before = lax.ppermute(last, axis, up)]
    dot_general x4 -> x0, matrix products: 9.54 us -> none  [spatial(): jnp.einsum('cwnsi,nsij->cwnj', blocks_of, masked, precision=lax.Precision...]
    unnamed x17 -> x19, local copies, waits for them, and re-layouts: 1.04 us -> 8.35 us
    gather x4 -> x0, local copies, waits for them, and re-layouts: 5.04 us -> none  [spatial(): padded.reshape(cancers, weeks_here, rows_here + 4, width)]
  transfers between devices with their start and end apart: 16 -> 0, of which waited for: 10 -> 0; matrix products, arithmetic and copies ran while one was open for 1% -> 0% of each run, Pallas kernels for 0% -> 0%
where the time goes in v1:
time: 40.3 us; the launch traced here: 40 us
  Pallas kernels  31.7 us (79%)
  local copies, waits for them, and re-layouts  8.35 us (21%)
    pallas_call x1, Pallas kernels, by_site(): pl.pallas_call(functools.partial(site_kernel, peers, areas, per_chip, wee...  31.7 us
    unnamed x19, local copies, waits for them, and re-layouts  8.35 us

profile of v1, /device:TPU:0, one launch (start us, length us, event | category | flops | bytes accessed | tf_op | source)
XLA Modules:
  0.0 40.0 jit_solution(15870586987367943951)
XLA Ops:
  0.0 0.0 copy-start
  0.0 1.6 %copy-done = f32[8,4,128,128]{3,2,1,0:T(8,128)S(1)} copy-done((f32[8,4,128,128]{3,2,1,0:T(8,128)S(1)}, f32[8,4,128,128]{3,2,1,0:T(8,128)}, u32[]{:S(2)}) %copy-start) | copy-done | bytes 2097176
  1.6 0.0 copy-start.1
  1.6 0.9 %copy-done.1 = f32[24,2,1024]{2,1,0:T(2,128)S(1)} copy-done((f32[24,2,1024]{2,1,0:T(2,128)S(1)}, f32[24,2,1024]{2,1,0:T(2,128)}, u32[]{:S(2)}) %copy-start.1) | copy-done | bytes 196632
  2.5 0.0 copy-start.2
  2.5 0.9 %copy-done.2 = f32[24,2,1024]{2,1,0:T(2,128)S(1)} copy-done((f32[24,2,1024]{2,1,0:T(2,128)S(1)}, f32[24,2,1024]{2,1,0:T(2,128)}, u32[]{:S(2)}) %copy-start.2) | copy-done | bytes 196632
  3.4 0.0 copy-start.3
  3.4 0.9 %copy-done.3 = s32[24,2,1024]{2,1,0:T(2,128)S(1)} copy-done((s32[24,2,1024]{2,1,0:T(2,128)S(1)}, s32[24,2,1024]{2,1,0:T(2,128)}, u32[]{:S(2)}) %copy-start.3) | copy-done | bytes 196632
  4.4 0.0 copy-start.4
  4.4 0.7 %copy-done.4 = s32[8,4]{0,1:T(4,128)S(1)} copy-done((s32[8,4]{0,1:T(4,128)S(1)}, s32[8,4]{0,1:T(4,128)}, u32[]{:S(2)}) %copy-start.4) | copy-done | bytes 152
  5.1 0.0 copy-start.5
  5.1 0.7 %copy-done.5 = f32[24]{0:T(128)S(1)} copy-done((f32[24]{0:T(128)S(1)}, f32[24]{0:T(128)}, u32[]{:S(2)}) %copy-start.5) | copy-done | bytes 120
  5.7 0.0 copy-start.6
  5.7 0.7 %copy-done.6 = f32[24]{0:T(128)S(1)} copy-done((f32[24]{0:T(128)S(1)}, f32[24]{0:T(128)}, u32[]{:S(2)}) %copy-start.6) | copy-done | bytes 120
  6.4 0.0 copy-start.7
  6.4 0.7 %copy-done.7 = f32[24]{0:T(128)S(1)} copy-done((f32[24]{0:T(128)S(1)}, f32[24]{0:T(128)}, u32[]{:S(2)}) %copy-start.7) | copy-done | bytes 120
  7.0 0.0 copy-start.8
  7.0 0.7 %copy-done.8 = s32[8]{0:T(128)S(1)} copy-done((s32[8]{0:T(128)S(1)}, s32[8]{0:T(128)}, u32[]{:S(2)}) %copy-start.8) | copy-done | bytes 56
  7.7 31.7 %shard_map.91 = f32[384,128]{1,0:T(8,128)S(1)} custom-call(f32[384,128]{1,0:T(8,128)S(1)} %bitcast.22, f32[384,128]{1,0:T(8,128)S(1)} %bitcast.23, s32[384,128]{1,0:T(8,128)S(1)} %bitcast.24, f32[24]{0:T(128)S(1)} %copy-done.5, f32[24]{0:T(128)S(1)} %copy-done.6, f32[24]{0:T(128)S(1)} %copy-done.7, f32[8,4,128,128]{3,2,1,0:T(8,128)S(1)} %copy-done, ...), custom_call_target="tpu_custom_call" | custom-call | tf_op jit(solution)/shard_map/pallas_call | solution.py:336
  39.3 0.7 %copy.15 = f32[24,2,1024]{2,1,0:T(2,128)} copy(f32[24,2,1024]{2,1,0:T(2,128)S(1)} %bitcast.21) | data formatting | bytes 393216
Async XLA Ops:
  0.0 1.6 %copy-start = (f32[8,4,128,128]{3,2,1,0:T(8,128)S(1)}, f32[8,4,128,128]{3,2,1,0:T(8,128)}, u32[]{:S(2)}) copy-start(f32[8,4,128,128]{3,2,1,0:T(8,128)} %blocks.1) | copy-start | bytes 6291460
  1.6 0.9 %copy-start.1 = (f32[24,2,1024]{2,1,0:T(2,128)S(1)}, f32[24,2,1024]{2,1,0:T(2,128)}, u32[]{:S(2)}) copy-start(f32[24,2,1024]{2,1,0:T(2,128)} %param.9) | copy-start | bytes 589828
  2.5 0.9 %copy-start.2 = (f32[24,2,1024]{2,1,0:T(2,128)S(1)}, f32[24,2,1024]{2,1,0:T(2,128)}, u32[]{:S(2)}) copy-start(f32[24,2,1024]{2,1,0:T(2,128)} %param.10) | copy-start | bytes 589828
  3.4 0.9 %copy-start.3 = (s32[24,2,1024]{2,1,0:T(2,128)S(1)}, s32[24,2,1024]{2,1,0:T(2,128)}, u32[]{:S(2)}) copy-start(s32[24,2,1024]{2,1,0:T(2,128)} %param.11) | copy-start | bytes 589828
  4.4 0.7 %copy-start.4 = (s32[8,4]{0,1:T(4,128)S(1)}, s32[8,4]{0,1:T(4,128)}, u32[]{:S(2)}) copy-start(s32[8,4]{0,1:T(4,128)} %param.16) | copy-start | bytes 388
  5.1 0.7 %copy-start.5 = (f32[24]{0:T(128)S(1)}, f32[24]{0:T(128)}, u32[]{:S(2)}) copy-start(f32[24]{0:T(128)} %tau.1) | copy-start | bytes 292
  5.7 0.7 %copy-start.6 = (f32[24]{0:T(128)S(1)}, f32[24]{0:T(128)}, u32[]{:S(2)}) copy-start(f32[24]{0:T(128)} %phi_one.1) | copy-start | bytes 292
  6.4 0.7 %copy-start.7 = (f32[24]{0:T(128)S(1)}, f32[24]{0:T(128)}, u32[]{:S(2)}) copy-start(f32[24]{0:T(128)} %phi_two.1) | copy-start | bytes 292
  7.0 0.7 %copy-start.8 = (s32[8]{0:T(128)S(1)}, s32[8]{0:T(128)}, u32[]{:S(2)}) copy-start(s32[8]{0:T(128)} %slot_count.1) | copy-start | bytes 100

commit v2 on v1

--- a/solution.py
+++ b/solution.py
@@ -87,11 +87,12 @@
 
 def site_kernel(
     peers, areas, per_chip, weeks_here, rows_here, slot_total,
-    latent, log_offset, case_counts, tau, phi_one, phi_two, blocks, slot_index, slot_count,
+    latent_in, offset_in, counts_in, tau_in, one_in, two_in, blocks, slot_index, slot_count,
     out,
+    latent, log_offset, case_counts, tau, phi_one, phi_two,
     packed, field, matrix, wide, index_all, count_all,
     temporal_rows, operand, product, mean, direction, residual, search, outgoing, returned,
-    send_sem, recv_sem, matrix_sem, table_sem, back_sem, return_sem,
+    input_sem, send_sem, recv_sem, matrix_sem, table_sem, back_sem, return_sem,
 ):
     me = lax.axis_index("wk")
     half = lax.axis_index("ar")
@@ -108,15 +109,27 @@
             barrier, inc=1, device_id={"wk": other // areas, "ar": lax.rem(other, areas)}, device_id_type=MESH
         )
 
+    inputs = [
+        pltpu.make_async_copy(source, target, input_sem.at[n])
+        for n, (source, target) in enumerate(
+            (
+                (latent_in, latent), (offset_in, log_offset), (counts_in, case_counts),
+                (tau_in, tau), (one_in, phi_one), (two_in, phi_two),
+            )
+        )
+    ]
+    for copy in inputs:
+        copy.start()
     own_rows = pl.ds(half * rows_here, rows_here)
     own_matrix = pltpu.make_async_copy(blocks, matrix.at[own_rows], matrix_sem.at[0])
-    own_matrix.start()
     own_index = pltpu.make_async_copy(slot_index, index_all.at[half], table_sem.at[0])
-    own_index.start()
     own_count = pltpu.make_async_copy(slot_count, count_all.at[half], table_sem.at[1])
-    own_count.start()
-
-    for site in range(peers * per_chip):
+    for copy in (own_matrix, own_index, own_count):
+        copy.start()
+    for copy in inputs:
+        copy.wait()
+
+    def pack(site):
         for week in range(weeks_here):
             row = pl.ds(site * rows_here * weeks_here + week, rows_here, stride=weeks_here)
             now = latent[row, :]
@@ -124,6 +137,9 @@
             packed[site, 0, week] = now
             packed[site, 1, week] = rate
             packed[site, 2, week] = case_counts[row, :].astype(jnp.float32) - rate
+
+    for peer in range(peers):
+        pack(peer * per_chip)
 
     pl.semaphore_wait(barrier, peers * areas - 1)
 
@@ -168,6 +184,9 @@
             away()
 
     for j in range(per_chip):
+        if j > 0:
+            for peer in range(peers):
+                pack(peer * per_chip + j)
         for step in range(peers):
             scatter(j, step, True)
 
@@ -332,13 +351,15 @@
     tile = (weeks_here, rows_here, width)
     plane = pltpu.VMEM((weeks * rows, width), f32)
     dma = pltpu.SemaphoreType.DMA
-    vmem, smem = pl.BlockSpec(memory_space=pltpu.VMEM), pl.BlockSpec(memory_space=pltpu.SMEM)
+    flat = (cancers * rows_here * weeks_here, width)
+    scalars = pltpu.SMEM((cancers,), f32)
     result = pl.pallas_call(
         functools.partial(site_kernel, peers, areas, per_chip, weeks_here, rows_here, slot_total),
-        out_shape=jax.ShapeDtypeStruct((cancers * rows_here * weeks_here, width), f32),
-        in_specs=[vmem] * 3 + [smem] * 3 + [pl.BlockSpec(memory_space=pl.ANY)] + [smem] * 2,
-        out_specs=vmem,
+        out_shape=jax.ShapeDtypeStruct(flat, f32),
+        in_specs=[pl.BlockSpec(memory_space=pltpu.HBM)] * 9,
+        out_specs=pl.BlockSpec(memory_space=pltpu.VMEM),
         scratch_shapes=[
+            pltpu.VMEM(flat, f32), pltpu.VMEM(flat, f32), pltpu.VMEM(flat, jnp.int32), scalars, scalars, scalars,
             pltpu.VMEM((cancers, 3) + tile, f32),
             pltpu.VMEM((site_slots, peers, areas, 3) + tile, f32),
             pltpu.VMEM((rows, slot_total, width, width), f32),
@@ -350,6 +371,7 @@
             plane, plane, plane, plane, plane,
             pltpu.VMEM((site_slots, peers, areas) + tile, f32),
             pltpu.VMEM((cancers,) + tile, f32),
+            dma((6,)),
             dma((per_chip, peers)),
             dma((site_slots, peers, areas)),
             dma((3,)),
@@ -358,7 +380,7 @@
             dma((cancers,)),
         ],
         compiler_params=pltpu.CompilerParams(
-            collective_id=0, has_side_effects=True, vmem_limit_bytes=40 * 1024 * 1024
+            collective_id=0, has_side_effects=True, vmem_limit_bytes=60 * 1024 * 1024
         ),
     )(
         as_rows(latent), as_rows(log_offset), as_rows(case_counts), tau, phi_one, phi_two,

time: 40.3 us -> 33.5 us (0.83)
  local copies, waits for them, and re-layouts: 8.35 us -> 1.62 us
    unnamed x19 -> x1, local copies, waits for them, and re-layouts: 8.35 us -> 1.62 us
where the time goes in v2:
time: 33.5 us; the launch traced here: 33.3 us
  Pallas kernels  31.7 us (95%)
  local copies, waits for them, and re-layouts  1.62 us (5%)
    pallas_call x1, Pallas kernels, by_site(): pl.pallas_call(functools.partial(site_kernel, peers, areas, per_chip, wee...  31.7 us
    unnamed x1, local copies, waits for them, and re-layouts  1.62 us

profile of v2, /device:TPU:0, one launch (start us, length us, event | category | flops | bytes accessed | tf_op | source)
XLA Modules:
  0.0 33.3 jit_solution(7030187501682894413)
XLA Ops:
  0.0 31.7 %shard_map.91 = f32[384,128]{1,0:T(8,128)} custom-call(f32[384,128]{1,0:T(8,128)} %bitcast.22, f32[384,128]{1,0:T(8,128)} %bitcast.23, s32[384,128]{1,0:T(8,128)} %bitcast.24, f32[24]{0:T(128)} %tau_in.1, f32[24]{0:T(128)} %one_in.1, f32[24]{0:T(128)} %two_in.1, f32[8,4,128,128]{3,2,1,0:T(8,128)} %blocks.1, s32[4,8]{1,0:T(4,128)} %bitcast.25, s32[8]{0:T(128)} %slot_count.1), custom_call_target="tpu_custom_call" | custom-call | tf_op jit(solution)/shard_map/pallas_call | solution.py:356
  31.7 1.6 %copy.15 = f32[24,2,1024]{2,1,0:T(2,128)} copy(f32[24,2,1024]{2,1,0:T(2,128)} %bitcast.21) | data formatting | bytes 393216

commit v3 on v2

--- a/solution.py
+++ b/solution.py
@@ -92,7 +92,7 @@
     latent, log_offset, case_counts, tau, phi_one, phi_two,
     packed, field, matrix, wide, index_all, count_all,
     temporal_rows, operand, product, mean, direction, residual, search, outgoing, returned,
-    input_sem, send_sem, recv_sem, matrix_sem, table_sem, back_sem, return_sem,
+    input_sem, send_sem, recv_sem, matrix_sem, table_sem, back_sem, return_sem, known_sem,
 ):
     me = lax.axis_index("wk")
     half = lax.axis_index("ar")
@@ -102,12 +102,34 @@
     rows = areas * rows_here
     sites_here = jnp.minimum(site_slots, per_chip - half * site_slots)
 
+    levels = peers // 2
+    level, column = me // 2, lax.rem(me, 2)
+    above, below = levels - 1 - level, level
     barrier = pltpu.get_barrier_semaphore()
-    for step in range(1, peers * areas):
-        other = lax.rem(me * areas + half + step, peers * areas)
-        pl.semaphore_signal(
-            barrier, inc=1, device_id={"wk": other // areas, "ar": lax.rem(other, areas)}, device_id_type=MESH
-        )
+
+    def where_level(far, act):
+        if far == 0:
+            act()
+        else:
+            pl.when(above >= far if far > 0 else below >= -far)(act)
+
+    for far in (1, -1, 0):
+
+        def greet(far=far):
+            for x in range(2):
+                for a in range(areas):
+
+                    def call():
+                        pl.semaphore_signal(
+                            barrier, inc=1, device_id={"wk": (level + far) * 2 + x, "ar": a}, device_id_type=MESH
+                        )
+
+                    if far == 0:
+                        pl.when(column * areas + half != x * areas + a)(call)
+                    else:
+                        call()
+
+        where_level(far, greet)
 
     inputs = [
         pltpu.make_async_copy(source, target, input_sem.at[n])
@@ -135,13 +157,36 @@
             now = latent[row, :]
             rate = jnp.exp(log_offset[row, :] + now)
             packed[site, 0, week] = now
-            packed[site, 1, week] = rate
-            packed[site, 2, week] = case_counts[row, :].astype(jnp.float32) - rate
+            packed[site, 1, week] = case_counts[row, :].astype(jnp.float32) - rate
+            packed[site, 2, week] = rate
 
     for peer in range(peers):
         pack(peer * per_chip)
 
-    pl.semaphore_wait(barrier, peers * areas - 1)
+    pl.semaphore_wait(
+        barrier, 2 * areas * (1 + jnp.minimum(above, 1) + jnp.minimum(below, 1)) - 1
+    )
+
+    def pass_on(far):
+        for row, sign in enumerate((1, -1)):
+            ahead, behind = (above, below) if sign > 0 else (below, above)
+
+            @pl.when(jnp.minimum(ahead - far, behind - 1) >= 0)
+            def _():
+                pl.semaphore_signal(
+                    known_sem.at[row, far], inc=1,
+                    device_id={"wk": (level - sign) * 2 + column}, device_id_type=MESH,
+                )
+
+    def learn(far):
+        for row, ahead in enumerate((above, below)):
+
+            @pl.when(ahead >= far)
+            def _():
+                pl.semaphore_wait(known_sem.at[row, far - 1], 1)
+
+    if levels > 2:
+        pass_on(1)
 
     twin = {"ar": 1 - half}
     twin_rows = pl.ds((1 - half) * rows_here, rows_here)
@@ -156,39 +201,58 @@
             blocks, matrix.at[own_rows], matrix_sem.at[1], matrix_sem.at[2], device_id=twin, device_id_type=MESH
         ),
     ]
+
+    def scatter(j, part, far, starting):
+        core, slot = j // site_slots, j % site_slots
+        halves = pl.ds(0, 2) if part == 0 else pl.ds(2, 1)
+
+        def across():
+            for x in range(2):
+                peer = (level + far) * 2 + x
+                source = packed.at[peer * per_chip + j, halves]
+                target, arrived = field.at[slot, me, half, halves], recv_sem.at[slot, me, half, part]
+
+                def away():
+                    copy = pltpu.make_async_remote_copy(
+                        source, target, send_sem.at[j, part, far + levels - 1, x], arrived,
+                        device_id={"wk": peer, "ar": core}, device_id_type=MESH,
+                    )
+                    copy.start() if starting else copy.wait_send()
+
+                def here():
+                    pltpu.make_async_copy(source, target, arrived).start()
+
+                if far == 0:
+                    mine = column * areas + half == x * areas + core
+                    pl.when(jnp.logical_not(mine))(away)
+                    if starting:
+                        pl.when(mine)(here)
+                else:
+                    away()
+
+        where_level(far, across)
+
+    def both_ways(far):
+        return (far, -far) if far else (0,)
+
+    for far in range(levels):
+        if far >= 2:
+            learn(far)
+            if far < levels - 1:
+                pass_on(far)
+        for way in both_ways(far):
+            scatter(0, 0, way, True)
     for copy in to_twin:
         copy.start()
-
-    def scatter(j, step, starting):
-        core, slot = j // site_slots, j % site_slots
-        peer = lax.rem(me + step, peers)
-        site = peer * per_chip + j
-        source, target = packed.at[site], field.at[slot, me, half]
-        arrived = recv_sem.at[slot, me, half]
-
-        def away():
-            copy = pltpu.make_async_remote_copy(
-                source, target, send_sem.at[j, step], arrived,
-                device_id={"wk": peer, "ar": core}, device_id_type=MESH,
-            )
-            copy.start() if starting else copy.wait_send()
-
-        def here():
-            pltpu.make_async_copy(source, target, arrived).start()
-
-        if step == 0:
-            pl.when(half != core)(away)
-            if starting:
-                pl.when(half == core)(here)
-        else:
-            away()
-
-    for j in range(per_chip):
-        if j > 0:
-            for peer in range(peers):
-                pack(peer * per_chip + j)
-        for step in range(peers):
-            scatter(j, step, True)
+    far_first = [way for far in range(levels - 1, -1, -1) for way in both_ways(far)]
+    for way in far_first:
+        scatter(0, 1, way, True)
+    for j in range(1, per_chip):
+        for peer in range(peers):
+            pack(peer * per_chip + j)
+        for part in range(2):
+            for way in far_first:
+                scatter(j, part, way, True)
 
     def spread(block_row):
         for slot in range(slot_total):
@@ -247,69 +311,91 @@
     def total(values):
         return jnp.sum(values, axis=(0, 1), keepdims=True)
 
-    def give(slot, step, a, starting):
-        peer = lax.rem(me + step, peers)
-        source = outgoing.at[slot, peer, a]
+    def give(slot, far, starting):
         site = me * per_chip + half * site_slots + slot
         target, arrived = returned.at[site], return_sem.at[site]
 
-        def away():
-            copy = pltpu.make_async_remote_copy(
-                source, target, back_sem.at[slot, step, a], arrived,
-                device_id={"wk": peer, "ar": a}, device_id_type=MESH,
-            )
-            copy.start() if starting else copy.wait_send()
-
-        def here():
-            pltpu.make_async_copy(source, target, arrived).start()
-
-        if step == 0:
-            pl.when(half != a)(away)
-            if starting:
-                pl.when(half == a)(here)
-        else:
-            away()
+        def across():
+            for x in range(2):
+                for a in range(areas):
+                    peer = (level + far) * 2 + x
+                    source = outgoing.at[slot, peer, a]
+
+                    def away():
+                        copy = pltpu.make_async_remote_copy(
+                            source, target, back_sem.at[slot, far + levels - 1, x, a], arrived,
+                            device_id={"wk": peer, "ar": a}, device_id_type=MESH,
+                        )
+                        copy.start() if starting else copy.wait_send()
+
+                    def here():
+                        pltpu.make_async_copy(source, target, arrived).start()
+
+                    if far == 0:
+                        mine = column * areas + half == x * areas + a
+                        pl.when(jnp.logical_not(mine))(away)
+                        if starting:
+                            pl.when(mine)(here)
+                    else:
+                        away()
+
+        where_level(far, across)
+
+    def take(slot, part):
+        halves = pl.ds(0, 2) if part == 0 else pl.ds(2, 1)
+        for w in range(peers):
+            for a in range(areas):
+                pltpu.make_async_copy(
+                    packed.at[0, halves], field.at[slot, w, a, halves], recv_sem.at[slot, w, a, part]
+                ).wait()
+
+    def unpack(slot, number, target):
+        for w in range(peers):
+            for a in range(areas):
+                for t in range(weeks_here):
+                    row = pl.ds((w * weeks_here + t) * rows + a * rows_here, rows_here)
+                    target[row, :] = field[slot, w, a, number, t]
 
     @pl.loop(0, sites_here)
     def _(slot):
         site = me * per_chip + half * site_slots + slot
         scale, first_lag, second_lag = tau[site], phi_one[site], phi_two[site]
-        for w in range(peers):
-            for a in range(areas):
-                pltpu.make_async_copy(packed.at[0], field.at[slot, w, a], recv_sem.at[slot, w, a]).wait()
-        for w in range(peers):
-            for a in range(areas):
-                for t in range(weeks_here):
-                    row = pl.ds((w * weeks_here + t) * rows + a * rows_here, rows_here)
-                    direction[row, :] = field[slot, w, a, 0, t]
-                    mean[row, :] = field[slot, w, a, 1, t]
-                    residual[row, :] = field[slot, w, a, 2, t]
+        take(slot, 0)
+        unpack(slot, 0, direction)
+        unpack(slot, 1, residual)
         prior(first_lag, second_lag)
         gradient = residual[...] - scale * product[...]
         residual[...] = gradient
         direction[...] = gradient
         search[...] = jnp.zeros_like(gradient)
+        prior(first_lag, second_lag)
+        take(slot, 1)
+        unpack(slot, 2, mean)
+
+        def step_length(norm_now):
+            image = scale * product[...] + mean[...] * direction[...]
+            return image, norm_now / total(direction[...] * image)
 
         def iteration(_, norm_now):
-            prior(first_lag, second_lag)
-            image = scale * product[...] + mean[...] * direction[...]
-            alpha = norm_now / total(direction[...] * image)
+            image, alpha = step_length(norm_now)
             search[...] += alpha * direction[...]
             after = residual[...] - alpha * image
             residual[...] = after
             norm_next = total(after * after)
             direction[...] = after + (norm_next / norm_now) * direction[...]
+            prior(first_lag, second_lag)
             return norm_next
 
-        lax.fori_loop(0, ITERS, iteration, total(gradient * gradient))
+        norm_last = lax.fori_loop(0, ITERS - 1, iteration, total(gradient * gradient))
+        _, alpha = step_length(norm_last)
+        search[...] += alpha * direction[...]
         for w in range(peers):
             for a in range(areas):
                 for t in range(weeks_here):
                     row = pl.ds((w * weeks_here + t) * rows + a * rows_here, rows_here)
                     outgoing[slot, w, a, t] = search[row, :]
-        for step in range(peers):
-            for a in range(areas):
-                give(slot, step, a, True)
+        for way in far_first:
+            give(slot, way, True)
 
     for j in range(per_chip):
         for w in range(peers):
@@ -322,14 +408,14 @@
     for copy in to_twin:
         copy.wait_send()
     for j in range(per_chip):
-        for step in range(peers):
-            scatter(j, step, False)
+        for part in range(2):
+            for way in far_first:
+                scatter(j, part, way, False)
 
     @pl.loop(0, sites_here)
     def _(slot):
-        for step in range(peers):
-            for a in range(areas):
-                give(slot, step, a, False)
+        for way in far_first:
+            give(slot, way, False)
 
 
 def by_site(
@@ -337,7 +423,7 @@
 ):
     cancers, weeks_here, areas_here = latent.shape
     rows_here, slot_total, width, _ = blocks.shape
-    if cancers % peers or areas != 2 or rows_here % 8 or (peers * weeks_here) % 16:
+    if cancers % peers or peers % 2 or areas != 2 or rows_here % 8 or (peers * weeks_here) % 16:
         return local(latent, log_offset, case_counts, tau, phi_one, phi_two, blocks, block_index, block_count)
     per_chip = cancers // peers
     site_slots = -(-per_chip // areas)
@@ -372,12 +458,13 @@
             pltpu.VMEM((site_slots, peers, areas) + tile, f32),
             pltpu.VMEM((cancers,) + tile, f32),
             dma((6,)),
-            dma((per_chip, peers)),
-            dma((site_slots, peers, areas)),
+            dma((per_chip, 2, peers - 1, 2)),
+            dma((site_slots, peers, areas, 2)),
             dma((3,)),
             dma((6,)),
-            dma((site_slots, peers, areas)),
+            dma((site_slots, peers - 1, 2, areas)),
             dma((cancers,)),
+            pltpu.SemaphoreType.REGULAR((2, peers // 2)),
         ],
         compiler_params=pltpu.CompilerParams(
             collective_id=0, has_side_effects=True, vmem_limit_bytes=60 * 1024 * 1024

time: 33.5 us -> 32.5 us (0.970)
  Pallas kernels: 31.7 us -> 30.7 us
    pallas_call x1, Pallas kernels: 31.7 us -> 30.7 us  [by_site(): pl.pallas_call(functools.partial(site_kernel, peers, areas, per_chip, wee...]
where the time goes in v3:
time: 32.5 us; the launch traced here: 32.3 us
  Pallas kernels  30.7 us (94%)
  local copies, waits for them, and re-layouts  1.62 us (5%)
    pallas_call x1, Pallas kernels, by_site(): pl.pallas_call(functools.partial(site_kernel, peers, areas, per_chip, wee...  30.7 us
    unnamed x1, local copies, waits for them, and re-layouts  1.62 us

profile of v3, /device:TPU:0, one launch (start us, length us, event | category | flops | bytes accessed | tf_op | source)
XLA Modules:
  0.0 32.3 jit_solution(12409808017346168164)
XLA Ops:
  0.0 30.7 %shard_map.91 = f32[384,128]{1,0:T(8,128)} custom-call(f32[384,128]{1,0:T(8,128)} %bitcast.22, f32[384,128]{1,0:T(8,128)} %bitcast.23, s32[384,128]{1,0:T(8,128)} %bitcast.24, f32[24]{0:T(128)} %tau_in.1, f32[24]{0:T(128)} %one_in.1, f32[24]{0:T(128)} %two_in.1, f32[8,4,128,128]{3,2,1,0:T(8,128)} %blocks.1, s32[4,8]{1,0:T(4,128)} %bitcast.25, s32[8]{0:T(128)} %slot_count.1), custom_call_target="tpu_custom_call" | custom-call | tf_op jit(solution)/shard_map/pallas_call | solution.py:442
  30.7 1.6 %copy.15 = f32[24,2,1024]{2,1,0:T(2,128)} copy(f32[24,2,1024]{2,1,0:T(2,128)} %bitcast.21) | data formatting | bytes 393216

commit v4 on v3

--- a/solution.py
+++ b/solution.py
@@ -439,9 +439,13 @@
     dma = pltpu.SemaphoreType.DMA
     flat = (cancers * rows_here * weeks_here, width)
     scalars = pltpu.SMEM((cancers,), f32)
+    operands = (
+        as_rows(latent), as_rows(log_offset), as_rows(case_counts), tau, phi_one, phi_two,
+        blocks, block_index.T, block_count,
+    )
     result = pl.pallas_call(
         functools.partial(site_kernel, peers, areas, per_chip, weeks_here, rows_here, slot_total),
-        out_shape=jax.ShapeDtypeStruct(flat, f32),
+        out_shape=pltpu.VMEM(flat, f32),
         in_specs=[pl.BlockSpec(memory_space=pltpu.HBM)] * 9,
         out_specs=pl.BlockSpec(memory_space=pltpu.VMEM),
         scratch_shapes=[
@@ -467,12 +471,9 @@
             pltpu.SemaphoreType.REGULAR((2, peers // 2)),
         ],
         compiler_params=pltpu.CompilerParams(
-            collective_id=0, has_side_effects=True, vmem_limit_bytes=60 * 1024 * 1024
+            collective_id=0, has_side_effects=True, vmem_limit_bytes=40 * 1024 * 1024
         ),
-    )(
-        as_rows(latent), as_rows(log_offset), as_rows(case_counts), tau, phi_one, phi_two,
-        blocks, block_index.T, block_count,
-    )
+    )(*(pltpu.with_memory_space_constraint(operand, pltpu.HBM) for operand in operands))
     split = result.reshape(cancers, rows_here, weeks_here, width).transpose(0, 2, 1, 3)
     return split.reshape(latent.shape)
 

time: 32.5 us -> 30.8 us (0.948)
  local copies, waits for them, and re-layouts: 1.62 us -> 0.68 us
  Pallas kernels: 30.7 us -> 30 us
    unnamed x1, local copies, waits for them, and re-layouts: 1.62 us -> 0.68 us
    pallas_call x1, Pallas kernels: 30.7 us -> 30 us  [by_site(): pl.pallas_call(functools.partial(site_kernel, peers, areas, per_chip, wee...]
where the time goes in v4:
time: 30.8 us; the launch traced here: 30.7 us
  Pallas kernels  30 us (97%)
  local copies, waits for them, and re-layouts  0.68 us (2%)
    pallas_call x1, Pallas kernels, by_site(): pl.pallas_call(functools.partial(site_kernel, peers, areas, per_chip, wee...  30 us
    unnamed x1, local copies, waits for them, and re-layouts  0.68 us

profile of v4, /device:TPU:0, one launch (start us, length us, event | category | flops | bytes accessed | tf_op | source)
XLA Modules:
  0.0 30.7 jit_solution(5869499518405746153)
XLA Ops:
  0.0 30.0 %shard_map.91 = f32[384,128]{1,0:T(8,128)S(1)} custom-call(f32[384,128]{1,0:T(8,128)} %bitcast.22, f32[384,128]{1,0:T(8,128)} %bitcast.23, s32[384,128]{1,0:T(8,128)} %bitcast.24, f32[24]{0:T(128)} %tau_in.1, f32[24]{0:T(128)} %one_in.1, f32[24]{0:T(128)} %two_in.1, f32[8,4,128,128]{3,2,1,0:T(8,128)} %blocks.1, s32[4,8]{1,0:T(4,128)} %bitcast.25, s32[8]{0:T(128)} %slot_count.1), custom_call_target="tpu_custom_call" | custom-call | tf_op jit(solution)/shard_map/pallas_call | solution.py:446
  30.0 0.7 %copy.15 = f32[24,2,1024]{2,1,0:T(2,128)} copy(f32[24,2,1024]{2,1,0:T(2,128)S(1)} %bitcast.21) | data formatting | bytes 393216

commit v5 on v4

--- a/solution.py
+++ b/solution.py
@@ -204,7 +204,7 @@
 
     def scatter(j, part, far, starting):
         core, slot = j // site_slots, j % site_slots
-        halves = pl.ds(0, 2) if part == 0 else pl.ds(2, 1)
+        halves = pl.ds(part, 1)
 
         def across():
             for x in range(2):
@@ -247,10 +247,12 @@
     far_first = [way for far in range(levels - 1, -1, -1) for way in both_ways(far)]
     for way in far_first:
         scatter(0, 1, way, True)
+    for way in far_first:
+        scatter(0, 2, way, True)
     for j in range(1, per_chip):
         for peer in range(peers):
             pack(peer * per_chip + j)
-        for part in range(2):
+        for part in range(3):
             for way in far_first:
                 scatter(j, part, way, True)
 
@@ -342,7 +344,7 @@
         where_level(far, across)
 
     def take(slot, part):
-        halves = pl.ds(0, 2) if part == 0 else pl.ds(2, 1)
+        halves = pl.ds(part, 1)
         for w in range(peers):
             for a in range(areas):
                 pltpu.make_async_copy(
@@ -362,14 +364,15 @@
         scale, first_lag, second_lag = tau[site], phi_one[site], phi_two[site]
         take(slot, 0)
         unpack(slot, 0, direction)
+        prior(first_lag, second_lag)
+        take(slot, 1)
         unpack(slot, 1, residual)
-        prior(first_lag, second_lag)
         gradient = residual[...] - scale * product[...]
         residual[...] = gradient
         direction[...] = gradient
         search[...] = jnp.zeros_like(gradient)
         prior(first_lag, second_lag)
-        take(slot, 1)
+        take(slot, 2)
         unpack(slot, 2, mean)
 
         def step_length(norm_now):
@@ -408,7 +411,7 @@
     for copy in to_twin:
         copy.wait_send()
     for j in range(per_chip):
-        for part in range(2):
+        for part in range(3):
             for way in far_first:
                 scatter(j, part, way, False)
 
@@ -462,8 +465,8 @@
             pltpu.VMEM((site_slots, peers, areas) + tile, f32),
             pltpu.VMEM((cancers,) + tile, f32),
             dma((6,)),
-            dma((per_chip, 2, peers - 1, 2)),
-            dma((site_slots, peers, areas, 2)),
+            dma((per_chip, 3, peers - 1, 2)),
+            dma((site_slots, peers, areas, 3)),
             dma((3,)),
             dma((6,)),
             dma((site_slots, peers - 1, 2, areas)),

time: 30.8 us -> 32.6 us (1.058)
  Pallas kernels: 30 us -> 31.8 us
    pallas_call x1, Pallas kernels: 30 us -> 31.8 us  [by_site(): pl.pallas_call(functools.partial(site_kernel, peers, areas, per_chip, wee...]
where the time goes in v5:
time: 32.6 us; the launch traced here: 32.5 us
  Pallas kernels  31.8 us (98%)
  local copies, waits for them, and re-layouts  0.68 us (2%)
    pallas_call x1, Pallas kernels, by_site(): pl.pallas_call(functools.partial(site_kernel, peers, areas, per_chip, wee...  31.8 us
    unnamed x1, local copies, waits for them, and re-layouts  0.68 us

profile of v5, /device:TPU:0, one launch (start us, length us, event | category | flops | bytes accessed | tf_op | source)
XLA Modules:
  0.0 32.5 jit_solution(12725427493020879789)
XLA Ops:
  0.0 31.8 %shard_map.91 = f32[384,128]{1,0:T(8,128)S(1)} custom-call(f32[384,128]{1,0:T(8,128)} %bitcast.22, f32[384,128]{1,0:T(8,128)} %bitcast.23, s32[384,128]{1,0:T(8,128)} %bitcast.24, f32[24]{0:T(128)} %tau_in.1, f32[24]{0:T(128)} %one_in.1, f32[24]{0:T(128)} %two_in.1, f32[8,4,128,128]{3,2,1,0:T(8,128)} %blocks.1, s32[4,8]{1,0:T(4,128)} %bitcast.25, s32[8]{0:T(128)} %slot_count.1), custom_call_target="tpu_custom_call" | custom-call | tf_op jit(solution)/shard_map/pallas_call | solution.py:449
  31.8 0.7 %copy.15 = f32[24,2,1024]{2,1,0:T(2,128)} copy(f32[24,2,1024]{2,1,0:T(2,128)S(1)} %bitcast.21) | data formatting | bytes 393216
